TPU v7x, 32 devices: a whole 2x2x4 slice. The times are simulated.
32 devices in a mesh: groups: 2 (over y), seq: 4 (over z), mp: 2 (over x), batch: 2 (over core).
Axes of the slice: x: 2, y: 2, z: 4, core: 2. Of those that a mesh axis runs over, the one named last changes fastest.
Arguments:
- hidden: bfloat16 [4, 1024, 2048], P(('groups', 'batch'), 'seq', 'mp'), parts along dimension 0, may hold values from -6 to 6
- segment_ids: int32 [4, 1024], P(('groups', 'batch'), 'seq'), parts along dimension 0, may hold values from 0 to 3, never falling along the last dimension, each value on 1 to 512 neighbouring positions
- norm_gain: float32 [2048], replicated, may hold values from 0.1 to 1.9
- w_gate: bfloat16 [2048, 2048], P('seq', 'mp'), may hold values from -0.125 to 0.125
- w_value: bfloat16 [2048, 2048], P('seq', 'mp'), may hold values from -0.125 to 0.125
- w_in_out: bfloat16 [2048, 256], P('seq', 'mp'), may hold values from -0.125 to 0.125
- w_step: bfloat16 [2048, 32], P('seq', 'mp'), may hold values from -0.125 to 0.125
- step_bias: float32 [32], P('mp'), may hold values from -3 to -1
- decay_rate: float32 [32], P('mp'), may hold values from 0 to 1, as said below
- skip_gain: float32 [32], P('mp'), may hold values from 0.5 to 1.5
- conv_value: bfloat16 [4, 2048], P(None, 'mp'), may hold values from -3 to 3
- conv_in_out: bfloat16 [4, 256], P(None, 'mp'), may hold values from -3 to 3
- w_out: bfloat16 [2048, 2048], P('mp', 'seq'), may hold values from -0.125 to 0.125
Outputs:
- mixed_out: bfloat16 [4, 1024, 2048], P(('groups', 'batch'), 'seq', 'mp'), parts along dimension 0
There are 2 independent parts, one for each index of `groups`. A program takes and returns all parts, laid end to end along the dimension named above; an argument that names none is the same for every part. Nothing has to cross between parts.
Inputs may be any that keep to these rules, and one draw needn't show every extreme that they name: `decay_rate`: each head's rate is positive and at most 0.15.
All inputs are finite; a program needn't handle non-finite values.
Results may differ from a plain program's by a relative error of at most 0.0076.
Values may be sent and summed in bfloat16 or wider, within the bound.
A program may use at most 64 MiB of HBM per device.

v0:
```python
import jax
import jax.numpy as jnp
from jax import lax
from jax.sharding import PartitionSpec as P

SPAN = 256
GROUP_HEADS = 8


def with_halo(block, sides, width):
    for axis, dim in sides:
        count = lax.axis_size(axis)
        forward = [(i, i + 1) for i in range(count - 1)]
        backward = [(target, source) for source, target in forward]
        low = lax.ppermute(
            lax.slice_in_dim(block, block.shape[dim] - width, None, axis=dim), axis, forward
        )
        high = lax.ppermute(lax.slice_in_dim(block, 0, width, axis=dim), axis, backward)
        block = jnp.concatenate([low, block, high], axis=dim)
    return block


def passed_along(value, axis, by):
    size = lax.axis_size(axis)
    pairs = [(i, i + by) for i in range(size) if 0 <= i + by < size]
    return lax.ppermute(value, axis, pairs)


def entering(value, axis, combine, identity, reverse):
    size, index = (lax.axis_size(axis), lax.axis_index(axis))
    everything = jax.tree.map(
        lambda part, kind: lax.all_gather(part.astype(kind), axis),
        value,
        (jnp.bfloat16, jnp.bfloat16),
    )
    start = jax.tree.map(
        lambda part, zero: jnp.broadcast_to(jnp.asarray(zero, part.dtype), part.shape),
        value,
        identity,
    )

    def lap(k, before):
        at = size - 1 - k if reverse else k
        reached = at > index if reverse else at < index
        new = combine(
            before, jax.tree.map(lambda part, own: part[at].astype(own.dtype), everything, value)
        )
        return jax.tree.map(lambda a, b: jnp.where(reached, a, b), new, before)

    return lax.fori_loop(0, size, lap, start)


def span_terms(values, input_maps, output_maps, log_decay, step_size, segment, segment_before):
    span_rows = values.shape[0]
    cumulative = jnp.cumsum(log_decay, axis=0)
    scores = jnp.dot(output_maps, input_maps.T, preferred_element_type=jnp.float32)
    row_index = lax.broadcasted_iota(jnp.int32, (span_rows, span_rows), 0)
    col_index = lax.broadcasted_iota(jnp.int32, (span_rows, span_rows), 1)
    allowed = (segment[:, None] == segment[None, :]) & (col_index <= row_index)
    cum_heads = cumulative.T
    spread = cum_heads[:, :, None] - cum_heads[:, None, :]
    weights = jnp.where(allowed[None], jnp.exp(jnp.where(allowed[None], spread, 0.0)), 0.0)
    mixing = (scores[None] * weights * step_size.T[:, None, :]).astype(jnp.bfloat16)
    intra_part = jnp.einsum("hij,jhp->ihp", mixing, values, preferred_element_type=jnp.float32)
    final_cum = cumulative[-1]
    same_end = (segment == segment[-1]).astype(jnp.float32)
    to_end = jnp.exp(final_cum[None] - cumulative) * step_size * same_end[:, None]
    weighted = (values.astype(jnp.float32) * to_end[:, :, None]).astype(jnp.bfloat16)
    span_state = jnp.einsum("jhp,jn->hpn", weighted, input_maps, preferred_element_type=jnp.float32)
    inflow = jnp.exp(cumulative) * (segment == segment_before).astype(jnp.float32)[:, None]
    passing = jnp.exp(final_cum) * (segment[-1] == segment_before).astype(jnp.float32)
    return (intra_part, span_state, inflow, passing)


def causal_conv(series, prior_rows, kernel):
    length_rows = series.shape[1]
    padded = jnp.concatenate([prior_rows, series], 1).astype(jnp.float32)
    summed = jnp.zeros(series.shape, jnp.float32)
    for tap_index in range(kernel.shape[0]):
        summed = (
            summed
            + kernel[tap_index].astype(jnp.float32) * padded[:, tap_index : tap_index + length_rows]
        )
    return jax.nn.silu(summed).astype(jnp.bfloat16)


def normalize(block_rows):
    widened = block_rows.astype(jnp.float32)
    return widened * lax.rsqrt(jnp.mean(widened * widened, axis=1, keepdims=True) + 1e-05)


def combine(earlier_part, later_part):
    return (
        earlier_part[0] * later_part[0],
        later_part[0][..., None, None] * earlier_part[1] + later_part[1],
    )


def compose(carried, inputs_pair):
    state_now, decay_now = carried
    span_state, span_pass = inputs_pair
    return (
        (span_pass[..., None, None] * state_now + span_state, decay_now * span_pass),
        (state_now, decay_now),
    )


def body(
    hidden,
    segment_ids,
    norm_gain,
    w_gate,
    w_value,
    w_in_out,
    w_step,
    step_bias,
    decay_rate,
    skip_gain,
    conv_value,
    conv_in_out,
    w_out,
):
    rows_local = hidden[0]
    segment = segment_ids[0]
    tok_count = rows_local.shape[0]
    extended = with_halo(segment, (("seq", 0),), 1)
    forward_full = lax.all_gather(rows_local, "mp", axis=1, tiled=True)
    reverse_full = forward_full[::-1]
    reverse_edges = extended[::-1]
    forward_in = (normalize(forward_full) * norm_gain).astype(jnp.bfloat16)
    reverse_in = (normalize(reverse_full)[:, ::-1] * norm_gain).astype(jnp.bfloat16)
    both_in = jnp.concatenate([forward_in, reverse_in], 0)
    pieces = (
        lax.all_gather(w_gate, "seq", axis=0, tiled=True),
        lax.all_gather(w_value, "seq", axis=0, tiled=True),
        lax.all_gather(w_in_out, "seq", axis=0, tiled=True),
        lax.all_gather(w_step, "seq", axis=0, tiled=True),
    )
    gate_sum, value_sum, inout_sum, step_sum = tuple(
        (jnp.dot(both_in, weight, preferred_element_type=jnp.float32) for weight in pieces)
    )
    gate_all = gate_sum.astype(jnp.bfloat16).reshape(2, tok_count, -1)
    value_pre = value_sum.astype(jnp.bfloat16).reshape(2, tok_count, -1)
    inout_pre = inout_sum.astype(jnp.bfloat16).reshape(2, tok_count, -1)
    reach_rows = conv_value.shape[0] - 1
    value_tail = value_pre[:, tok_count - reach_rows :]
    inout_tail = inout_pre[:, tok_count - reach_rows :]
    forward_prior = passed_along((value_tail[0], inout_tail[0]), "seq", 1)
    reverse_prior = passed_along((value_tail[1], inout_tail[1]), "seq", -1)
    value_prior = jnp.stack([forward_prior[0], reverse_prior[0]])
    inout_prior = jnp.stack([forward_prior[1], reverse_prior[1]])
    values_conv = causal_conv(value_pre, value_prior, conv_value)
    inout_conv = causal_conv(inout_pre, inout_prior, conv_in_out)
    inout_full = lax.all_gather(inout_conv, "mp", axis=2, tiled=True)
    state_width = inout_full.shape[2] // 2
    step_size = jax.nn.softplus(step_sum.reshape(2, tok_count, -1) + step_bias)
    log_decay = -step_size * decay_rate
    heads_local = step_size.shape[2]
    head_width = values_conv.shape[2] // heads_local
    count_spans = tok_count // SPAN
    segments_pair = jnp.stack([extended[1:-1], reverse_edges[1:-1]]).reshape(2, count_spans, SPAN)
    priors_pair = jnp.stack([extended[0], reverse_edges[0]])
    before_pair = jnp.concatenate([priors_pair[:, None], segments_pair[:, :-1, -1]], 1)
    span_values = values_conv.reshape(2, count_spans, SPAN, heads_local, head_width)
    span_inputs = inout_full[..., :state_width].reshape(2, count_spans, SPAN, state_width)
    span_outputs = inout_full[..., state_width:].reshape(2, count_spans, SPAN, state_width)
    span_logs = log_decay.reshape(2, count_spans, SPAN, heads_local)
    span_steps = step_size.reshape(2, count_spans, SPAN, heads_local)
    intra_part, states, inflow, passing = jax.vmap(jax.vmap(span_terms))(
        span_values, span_inputs, span_outputs, span_logs, span_steps, segments_pair, before_pair
    )
    start_pair = (
        jnp.zeros(states.shape[:1] + states.shape[2:], jnp.float32),
        jnp.ones((2, heads_local), jnp.float32),
    )
    summary_pair, before_parts = lax.scan(
        compose, start_pair, (jnp.moveaxis(states, 1, 0), jnp.moveaxis(passing, 1, 0))
    )
    summary_state, summary_decay = summary_pair
    before_states, before_decay = before_parts
    identity = (jnp.ones_like(summary_decay[0]), jnp.zeros_like(summary_state[0]))
    forward_entry = entering((summary_decay[0], summary_state[0]), "seq", combine, identity, False)
    reverse_entry = entering((summary_decay[1], summary_state[1]), "seq", combine, identity, True)
    entry_state = jnp.stack([forward_entry[1], reverse_entry[1]])
    span_entry = before_states + before_decay[..., None, None] * entry_state[None]
    span_entry = jnp.moveaxis(span_entry, 0, 1).astype(jnp.bfloat16)
    carried = jnp.einsum(
        "skin,skhpn->skihp", span_outputs, span_entry, preferred_element_type=jnp.float32
    )
    mixed = (
        intra_part
        + inflow[..., None] * carried
        + skip_gain[:, None] * span_values.astype(jnp.float32)
    )
    mixed = mixed.reshape(2, tok_count, heads_local * head_width)
    gate_wide = lax.optimization_barrier(gate_all).astype(jnp.float32)
    gated_out = mixed * jax.nn.silu(gate_wide)
    grouped = gated_out.reshape(2, tok_count, -1, GROUP_HEADS * head_width)
    normed = grouped * lax.rsqrt(jnp.mean(grouped * grouped, axis=3, keepdims=True) + 1e-05)
    normed = normed.reshape(2, tok_count, heads_local * head_width).astype(jnp.bfloat16)
    forward_mix = normed[0]
    reverse_mix = normed[1][::-1]
    block_cols = lax.all_gather(w_out, "seq", axis=1, tiled=True)
    direct = jnp.dot(forward_mix, block_cols, preferred_element_type=jnp.float32)
    flipped = jnp.dot(reverse_mix, block_cols, preferred_element_type=jnp.float32)[:, ::-1]
    running = direct
    running = running + flipped
    result = lax.psum_scatter(running, "mp", scatter_dimension=1, tiled=True).astype(jnp.bfloat16)
    return result[None]


def solution(mesh):
    placed = (
        P(("groups", "batch"), "seq", "mp"),
        P(("groups", "batch"), "seq"),
        P(),
        P("seq", "mp"),
        P("seq", "mp"),
        P("seq", "mp"),
        P("seq", "mp"),
        P("mp"),
        P("mp"),
        P("mp"),
        P(None, "mp"),
        P(None, "mp"),
        P("mp", "seq"),
    )
    return jax.shard_map(
        body,
        mesh=mesh,
        in_specs=placed,
        out_specs=P(("groups", "batch"), "seq", "mp"),
        check_vma=False,
    )
```

profile of v0, /device:TPU:0, one launch (start us, length us, event | category | flops | bytes accessed | tf_op | source)
XLA Modules:
  0.0 399.6 jit_solution(7486551002777506659)
XLA Ops:
  8.1 1.3 fusion.48
  9.3 5.4 %collective-permute-start.4 = (s32[1]{0:T(128)}, s32[1]{0:T(128)}, u32[]{:S(2)}, u32[]{:S(2)}) collective-permute-start(s32[1]{0:T(128)} %bitcast.30), channel_id=1, source_target_pairs={{0,4},{4,8},{8,12},{1,5},{5,9},{9,13},{2,6},{6,10},{10,14},{3,7},{... | collective-permute-start | bytes 20 | tf_op jit(solution)/shard_map/ppermute | solution.py:15
  14.7 1.3 collective-permute-start.5
  16.1 14.1 %all_gather.41 = bf16[2048,16]{0,1:T(8,128)(2,1)S(1)} all-gather(bf16[512,16]{0,1:T(8,128)(2,1)S(1)} %copy-done.17), channel_id=1, replica_groups=mesh['groups'=2,'seq'=4,'mp'=2,'batch'=2] {'seq'}, dimensions={0}, use_global_device_ids=true | all-gather | bytes 81920 | tf_op jit(solution)/shard_map/all_gather | solution.py:137
  30.5 17.5 %all_gather.39 = bf16[2048,128]{1,0:T(8,128)(2,1)} all-gather(bf16[512,128]{1,0:T(8,128)(2,1)S(1)} %copy-done.12), channel_id=1, replica_groups=mesh['groups'=2,'seq'=4,'mp'=2,'batch'=2] {'seq'}, dimensions={0}, use_global_device_ids=true | all-gather | bytes 655360 | tf_op jit(solution)/shard_map/all_gather | solution.py:136
  48.1 1.3 pad_add_fusion.1
  49.4 1.4 fusion.38
  50.8 12.6 %rev.13 = bf16[256,2048]{1,0:T(8,128)(2,1)S(1)} reverse(bf16[256,2048]{1,0:T(8,128)(2,1)} %bitcast.139), dimensions={0} | reverse | bytes 2097152 | tf_op jit(solution)/shard_map/rev | solution.py:128
  63.7 1.6 convert_multiply_fusion.1
  65.3 15.0 %rev.14 = f32[256,2048]{1,0:T(8,128)S(1)} reverse(f32[256,2048]{1,0:T(8,128)} %convert_multiply_fusion.1), dimensions={1} | reverse | bytes 4194304 | tf_op jit(solution)/shard_map/rev | solution.py:131
  83.5 1.2 reduce-window.6
  85.1 2.4 convolution_convert_fusion.2
  87.5 4.0 collective-permute-start.2
  91.5 1.3 collective-permute-start.3
  94.4 3.9 collective-permute-done.3
  98.5 16.9 %all-gather.10.cloned.1.call-done = bf16[2048,1024]{1,0:T(8,128)(2,1)} async-done(((bf16[512,1024]{1,0:T(8,128)(2,1)}), bf16[2048,1024]{1,0:T(8,128)(2,1)}) %all-gather.10.cloned.1.call-update) | async-done | bytes 4194320 | tf_op jit(solution)/shard_map/all_gather | solution.py:135
  115.4 4.5 %convolution_convert_fusion.1 = bf16[512,1024]{1,0:T(8,128)(2,1)S(1)} fusion(bf16[2048,1024]{1,0:T(8,128)(2,1)} %all-gather.10.cloned.1.call-done, bf16[256,2048]{1,0:T(8,128)(2,1)S(1)} %copy-done.9, bf16[256,2048]{1,0:T(8,128)(2,1)S(1)} %copy-done.7), kind=kOutput, calls=%fused_computation.44 | convolution fusion | flops 2152202240 | bytes 7340032 | tf_op jit(solution)/shard_map/dot_general | solution.py:140
  119.9 2.1 collective-permute-start
  122.0 1.3 collective-permute-start.1
  123.3 5.8 %all_gather.40 = bf16[2,256,256]{2,1,0:T(8,128)(2,1)S(1)} all-gather(bf16[2,256,128]{2,1,0:T(8,128)(2,1)S(1)} %multiply_convert_fusion.9), channel_id=1, replica_groups=mesh['groups'=2,'seq'=4,'mp'=2,'batch'=2] {'mp'}, dimensions={2}, use_global_device_ids=true | all-gather | bytes 393216 | tf_op jit(solution)/shard_map/all_gather | solution.py:154
  129.4 1.3 multiply_convert_fusion.4
  134.1 11.3 %all-gather.1 = bf16[4,1,16]{2,1,0:T(2,128)(2,1)S(1)} all-gather(bf16[1,1,16]{2,1,0:T(2,128)(2,1)S(1)} %get-tuple-element.338), channel_id=3, replica_groups=mesh['groups'=2,'seq'=4,'mp'=2,'batch'=2] {'seq'}, dimensions={0}, use_global_device_ids=true | all-gather | bytes 160 | tf_op jit(solution)/shard_map/all_gather | solution.py:32
  145.5 8.4 %all-gather.2 = bf16[4,1,16]{2,1,0:T(2,128)(2,1)S(1)} all-gather(bf16[1,1,16]{2,1,0:T(2,128)(2,1)S(1)} %get-tuple-element.339), channel_id=4, replica_groups=mesh['groups'=2,'seq'=4,'mp'=2,'batch'=2] {'seq'}, dimensions={0}, use_global_device_ids=true | all-gather | bytes 160 | tf_op jit(solution)/shard_map/all_gather | solution.py:32
  155.6 41.3 %all-gather.16.cloned.1.call-done = bf16[2048,1024]{1,0:T(8,128)(2,1)} async-done(((bf16[512,1024]{1,0:T(8,128)(2,1)}), bf16[2048,1024]{1,0:T(8,128)(2,1)}) %all-gather.16.cloned.1.call-update) | async-done | bytes 4194320 | tf_op jit(solution)/shard_map/all_gather | solution.py:134
  196.9 5.2 %convolution_convert_fusion = bf16[512,1024]{1,0:T(8,128)(2,1)S(1)} fusion(bf16[2048,1024]{1,0:T(8,128)(2,1)} %all-gather.16.cloned.1.call-done, bf16[256,2048]{1,0:T(8,128)(2,1)} %copy-done.8, bf16[256,2048]{1,0:T(8,128)(2,1)} %copy-done.6), kind=kOutput, calls=%fused_computation.43 | convolution fusion | flops 2152202240 | bytes 7340032 | tf_op jit(solution)/shard_map/dot_general | solution.py:140
  202.1 1.7 copy.94
  203.7 21.1 %all-gather.12.cloned.1.call-done = bf16[4,16,64,128]{3,2,1,0:T(8,128)(2,1)} async-done(((bf16[1,16,64,128]{3,2,1,0:T(8,128)(2,1)}), bf16[4,16,64,128]{3,2,1,0:T(8,128)(2,1)}) %all-gather.12.cloned.1.call-update) | async-done | bytes 1048592 | tf_op jit(solution)/shard_map/all_gather | solution.py:32
  224.8 4.5 %while.37 = (s32[]{:T(128)}, f32[16,64,128]{2,1,0:T(8,128)S(1)}, s32[]{:T(128)}, bf16[4,16]{1,0:T(4,128)(2,1)S(1)}, bf16[4,16,64,128]{3,2,1,0:T(8,128)(2,1)}, /*index=5*/s32[]{:T(128)}, s32[]{:T(128)}) while((s32[]{:T(128)}, f32[16,64,128]{2,1,0:T(8,128)S(1)}, s32[]{:T(128)}, bf16[4,16]{1,0:T(4,128)(2,1)S(1)}, ...), condition=%wide.region_5.6_spmd.clone, body=%wide.region_4.5_spmd.clone.sunk | while | flops 655380 | bytes 1310985 | solution.py:50
  225.9 1.1 fusion.60
  229.3 24.4 %all-gather.14.cloned.1.call-done = bf16[4,16,64,128]{3,2,1,0:T(8,128)(2,1)} async-done(((bf16[1,16,64,128]{3,2,1,0:T(8,128)(2,1)}), bf16[4,16,64,128]{3,2,1,0:T(8,128)(2,1)}) %all-gather.14.cloned.1.call-update) | async-done | bytes 1048592 | tf_op jit(solution)/shard_map/all_gather | solution.py:32
  253.7 4.5 %while.38 = (s32[]{:T(128)}, f32[16,64,128]{2,1,0:T(8,128)S(1)}, s32[]{:T(128)}, bf16[4,16]{1,0:T(4,128)(2,1)S(1)}, bf16[4,16,64,128]{3,2,1,0:T(8,128)(2,1)}, /*index=5*/s32[]{:T(128)}, s32[]{:T(128)}, s32[]{:T(128)}, s32[]{:T(128)}) while((s32[]{:T(128)}, f32[16,64,128]{2,1,0:T(8,128)S(1)}, s32[]{:T(128)}, ...), condition=%wide.region_7.8_spmd.clone, body=%wide.region_6.7_spmd.clone.sunk | while | flops 655384 | bytes 1311047 | solution.py:50
  254.8 1.1 fusion.61
  256.0 1.1 fusion.61
  257.1 1.1 fusion.61
  260.2 4.3 %fusion.20 = f32[2,1,256,16,64]{2,4,3,0,1:T(8,128)} fusion(f32[2,1,256,16,64]{2,4,3,0,1:T(8,128)S(1)} %bitcast.142, f32[2,256,16,64]{1,3,2,0:T(8,128)S(1)} %fusion.23, bf16[2,256,16,64]{1,3,2,0:T(8,128)(2,1)S(1)} %bitcast.147, f32[2,16,256]{2,1,0:T(8,128)S(1)} %copy-done.16, f32[2,16,256]{2,1,0:T(8,128)S(1)} %copy-done.13, ...), kind=kOutput, calls=%fused_computation.38 | convolution fusion | flops 283115520 | bytes 8093760 | tf_op jit(solution)/shard_map/vmap(vmap(hij,jhp->ihp))/dot_general | solution.py:64
  264.5 2.0 copy.95
  266.5 2.0 fusion.45
  268.4 4.1 %mul.393 = f32[2,256,2,512]{3,2,1,0:T(2,128)} reshape(f32[2,256,1024]{2,1,0:T(8,128)} %fusion.45) | data formatting | bytes 4194304 | tf_op jit(solution)/shard_map/mul | solution.py:199
  272.5 2.2 reduce_sum.29
  274.8 1.7 mul.394
  276.6 4.1 %mul.395 = f32[2,256,1024]{2,1,0:T(8,128)} reshape(f32[2,256,2,512]{3,2,1,0:T(2,128)} %mul.394) | data formatting | bytes 4194304 | tf_op jit(solution)/shard_map/mul | solution.py:199
  280.7 2.4 multiply_convert_fusion.2
  284.7 50.7 %all-gather.18.cloned.1.call-done = bf16[1024,2048]{1,0:T(8,128)(2,1)} async-done(((bf16[1024,512]{1,0:T(8,128)(2,1)}), bf16[1024,2048]{1,0:T(8,128)(2,1)}) %all-gather.18.cloned.1.call-update) | async-done | bytes 4194320 | tf_op jit(solution)/shard_map/all_gather | solution.py:203
  335.4 4.8 %fusion.49 = f32[256,2048]{1,0:T(8,128)} fusion(bf16[256,1024]{1,0:T(8,128)(2,1)S(1)} %rev.15, bf16[1024,2048]{1,0:T(8,128)(2,1)} %all-gather.18.cloned.1.call-done), kind=kOutput, calls=%fused_computation.125 | convolution fusion | flops 1073741824 | bytes 6815744 | tf_op jit(solution)/shard_map/dot_general | solution.py:205
  340.2 15.0 %rev.16 = f32[256,2048]{1,0:T(8,128)S(1)} reverse(f32[256,2048]{1,0:T(8,128)} %fusion.49), dimensions={1} | reverse | bytes 4194304 | tf_op jit(solution)/shard_map/rev | solution.py:205
  355.2 4.8 %convolution_add_fusion = f32[256,2048]{1,0:T(8,128)} fusion(f32[256,2048]{1,0:T(8,128)S(1)} %rev.16, bf16[1024,2048]{1,0:T(8,128)(2,1)} %all-gather.18.cloned.1.call-done, bf16[2,256,1024]{2,1,0:T(8,128)(2,1)S(1)} %copy-done.2), kind=kOutput, calls=%fused_computation.20 | convolution fusion | flops 1074266112 | bytes 8912896 | tf_op jit(solution)/shard_map/dot_general | solution.py:204
  360.1 30.5 %reduce-scatter.2.cloned.1.call-done = f32[256,1024]{1,0:T(8,128)} async-done(((f32[256,2048]{1,0:T(8,128)}), f32[256,1024]{1,0:T(8,128)}) %reduce-scatter.2.cloned.1.call-update) | async-done | bytes 1048592 | tf_op jit(solution)/shard_map/reduce_scatter | solution.py:208
  390.6 2.1 convert_bitcast_fusion
  (133 shorter events, 20.9 us)
Async XLA Ops:
  6.5 23.6 %copy-start.18 = (s32[1,256]{1,0:T(1,128)S(1)}, s32[1,256]{1,0:T(1,128)}, u32[]{:S(2)}) copy-start(s32[1,256]{1,0:T(1,128)} %param.18) | copy-start | bytes 3076
  6.5 9.6 %copy-start.17 = (bf16[512,16]{0,1:T(8,128)(2,1)S(1)}, bf16[512,16]{0,1:T(8,128)(2,1)}, u32[]{:S(2)}) copy-start(bf16[512,16]{0,1:T(8,128)(2,1)} %param.23) | copy-start | bytes 49156
  6.5 23.9 %copy-start.12 = (bf16[512,128]{1,0:T(8,128)(2,1)S(1)}, bf16[512,128]{1,0:T(8,128)(2,1)}, u32[]{:S(2)}) copy-start(bf16[512,128]{1,0:T(8,128)(2,1)} %param.22) | copy-start | bytes 393220
  6.5 41.5 %copy-start.20 = (bf16[4,128]{1,0:T(4,128)(2,1)S(1)}, bf16[4,128]{1,0:T(4,128)(2,1)}, u32[]{:S(2)}) copy-start(bf16[4,128]{1,0:T(4,128)(2,1)} %param.28) | copy-start | bytes 3076
  6.5 41.5 %copy-start.14 = (bf16[4,1024]{1,0:T(4,128)(2,1)S(1)}, bf16[4,1024]{1,0:T(4,128)(2,1)}, u32[]{:S(2)}) copy-start(bf16[4,1024]{1,0:T(4,128)(2,1)} %param.27) | copy-start | bytes 24580
  6.5 44.2 %all-gather.20.cloned.1.call-start = ((), (), s32[]{:S(2)}) async-start(), calls=%async_computation.7 | async-start | bytes 1572864 | tf_op jit(solution)/shard_map/all_gather | solution.py:127
  7.3 108.1 %all-gather.10.cloned.1.call-start = ((), (), s32[]{:S(2)}) async-start(), calls=%async_computation.1 | async-start | bytes 5242880 | tf_op jit(solution)/shard_map/all_gather | solution.py:135
  8.0 188.9 %all-gather.16.cloned.1.call-start = ((), (), s32[]{:S(2)}) async-start(), calls=%async_computation.4 | async-start | bytes 5242880 | tf_op jit(solution)/shard_map/all_gather | solution.py:134
  9.3 38.7 %collective-permute-start.4 = (s32[1]{0:T(128)}, s32[1]{0:T(128)}, u32[]{:S(2)}, u32[]{:S(2)}) collective-permute-start(s32[1]{0:T(128)} %bitcast.30), channel_id=1, source_target_pairs={{0,4},{4,8},{8,12},{1,5},{5,9},{9,13},{2,6},{6,10},{10,14},{3,7},{... | collective-permute-start | bytes 20 | tf_op jit(solution)/shard_map/ppermute | solution.py:15
  14.7 33.3 %collective-permute-start.5 = (s32[1]{0:T(128)}, s32[1]{0:T(128)}, u32[]{:S(2)}, u32[]{:S(2)}) collective-permute-start(s32[1]{0:T(128)} %bitcast.31), channel_id=1, source_target_pairs={{4,0},{8,4},{12,8},{5,1},{9,5},{13,9},{6,2},{10,6},{14,10},{7,3},{... | collective-permute-start | bytes 20 | tf_op jit(solution)/shard_map/ppermute | solution.py:18
  16.0 208.8 %all-gather.12.cloned.1.call-start = ((), (), s32[]{:S(2)}) async-start(), calls=%async_computation.2 | async-start | bytes 1310720 | tf_op jit(solution)/shard_map/all_gather | solution.py:32
  65.3 15.0 %copy-start = (bf16[1,256,2048]{2,1,0:T(8,128)(2,1)S(1)}, bf16[1,256,2048]{2,1,0:T(8,128)(2,1)}, u32[]{:S(2)}) copy-start(bf16[1,256,2048]{2,1,0:T(8,128)(2,1)} %all-gather.20.cloned.1.call-done) | copy-start | bytes 3145732
  65.3 15.3 %copy-start.19 = (f32[2048]{0:T(1024)S(1)}, f32[2048]{0:T(1024)}, u32[]{:S(2)}) copy-start(f32[2048]{0:T(1024)} %param.19) | copy-start | bytes 24580
  81.2 1.0 copy-start.6
  81.2 1.4 copy-start.8
  81.2 2.1 copy-start.21
  81.2 2.1 copy-start.22
  82.6 2.5 copy-start.10
  85.1 30.3 %copy-start.7 = (bf16[256,2048]{1,0:T(8,128)(2,1)S(1)}, bf16[256,2048]{1,0:T(8,128)(2,1)}, u32[]{:S(2)}) copy-start(bf16[256,2048]{1,0:T(8,128)(2,1)} %copy-done.6) | copy-start | bytes 3145732
  85.1 30.3 %copy-start.9 = (bf16[256,2048]{1,0:T(8,128)(2,1)S(1)}, bf16[256,2048]{1,0:T(8,128)(2,1)}, u32[]{:S(2)}) copy-start(bf16[256,2048]{1,0:T(8,128)(2,1)} %copy-done.8) | copy-start | bytes 3145732
  87.5 6.9 %collective-permute-start.2 = (bf16[3,128]{1,0:T(4,128)(2,1)S(1)}, bf16[3,128]{1,0:T(4,128)(2,1)S(1)}, u32[]{:S(2)}, u32[]{:S(2)}) collective-permute-start(bf16[3,128]{1,0:T(4,128)(2,1)S(1)} %get-tuple-element.318), channel_id=1, source_target_pairs={{0,4},{4,8},{8,12},{1,5},{5,9},{9,13},{2,6},{6,10},{10,14},{3,7},{... | collective-permute-start | bytes 2312 | tf_op jit(solution)/shard_map/ppermute | solution.py:26
  91.5 6.7 %collective-permute-start.3 = (bf16[3,128]{1,0:T(4,128)(2,1)S(1)}, bf16[3,128]{1,0:T(4,128)(2,1)S(1)}, u32[]{:S(2)}, u32[]{:S(2)}) collective-permute-start(bf16[3,128]{1,0:T(4,128)(2,1)S(1)} %get-tuple-element.319), channel_id=1, source_target_pairs={{4,0},{8,4},{12,8},{5,1},{9,5},{13,9},{6,2},{10,6},{14,10},{7,3},{... | collective-permute-start | bytes 2312 | tf_op jit(solution)/shard_map/ppermute | solution.py:26
  119.9 9.2 %collective-permute-start = (bf16[3,1024]{1,0:T(4,128)(2,1)S(1)}, bf16[3,1024]{1,0:T(4,128)(2,1)S(1)}, u32[]{:S(2)}, u32[]{:S(2)}) collective-permute-start(bf16[3,1024]{1,0:T(4,128)(2,1)S(1)} %get-tuple-element.314), channel_id=1, source_target_pairs={{0,4},{4,8},{8,12},{1,5},{5,9},{9,13},{2,6},{6,10},{10,14},{3,7},{... | collective-permute-start | bytes 18440 | tf_op jit(solution)/shard_map/ppermute | solution.py:26
  122.0 7.1 %collective-permute-start.1 = (bf16[3,1024]{1,0:T(4,128)(2,1)S(1)}, bf16[3,1024]{1,0:T(4,128)(2,1)S(1)}, u32[]{:S(2)}, u32[]{:S(2)}) collective-permute-start(bf16[3,1024]{1,0:T(4,128)(2,1)S(1)} %get-tuple-element.315), channel_id=1, source_target_pairs={{4,0},{8,4},{12,8},{5,1},{9,5},{13,9},{6,2},{10,6},{14,10},{7,3},{... | collective-permute-start | bytes 18440 | tf_op jit(solution)/shard_map/ppermute | solution.py:26
  131.2 2.5 copy-start.4
  132.6 121.1 %all-gather.14.cloned.1.call-start = ((), (), s32[]{:S(2)}) async-start(), calls=%async_computation.3 | async-start | bytes 1310720 | tf_op jit(solution)/shard_map/all_gather | solution.py:32
  133.1 202.3 %all-gather.18.cloned.1.call-start = ((), (), s32[]{:S(2)}) async-start(), calls=%async_computation.5 | async-start | bytes 5242880 | tf_op jit(solution)/shard_map/all_gather | solution.py:203
  133.7 256.9 %reduce-scatter.2.cloned.1.call-start = ((), (), s32[]{:S(2)}) async-start(), calls=%async_computation.6 | async-start | bytes 3145728 | tf_op jit(solution)/shard_map/reduce_scatter | solution.py:208
  258.2 1.6 copy-start.3
  258.2 1.8 copy-start.5
  258.2 2.0 copy-start.11
  258.3 2.0 copy-start.13
  258.3 2.0 copy-start.15
  258.3 1.9 copy-start.16
  258.3 1.9 copy-start.23
  283.1 1.0 copy-start.1
  340.2 15.0 %copy-start.2 = (bf16[2,256,1024]{2,1,0:T(8,128)(2,1)S(1)}, bf16[2,256,1024]{2,1,0:T(8,128)(2,1)}, u32[]{:S(2)}) copy-start(bf16[2,256,1024]{2,1,0:T(8,128)(2,1)} %copy-done.1) | copy-start | bytes 3145732
Sparse Core Ops, SparseCore 0:
  8.9 23.9 all-gather.19
  34.5 80.8 all-gather.9
  117.0 79.8 all-gather.15
  198.3 26.4 all-gather.11
  226.2 27.4 all-gather.13
  255.1 80.2 all-gather.17
  360.2 30.3 reduce-scatter.1
where the time goes:
time: 403 us; the launch traced here: 400 us
  waiting for transfers between devices  191 us (47%)
  local copies, waits for them, and re-layouts  64.4 us (16%)
  blocking collectives  57.2 us (14%)
  matrix products  28.5 us (7%)
  other arithmetic  28.4 us (7%)
  starting transfers between devices  15.6 us (4%)
  between operations  14 us (3%)
    all_gather x1, waiting for transfers between devices, body(): block_cols = lax.all_gather(w_out, 'seq', axis=1, tiled=True)  50.7 us
    all_gather x2, waiting for transfers between devices, entering(): lax.all_gather(part.astype(kind), axis)  45.4 us
    all_gather x1, waiting for transfers between devices, body(): lax.all_gather(w_gate, 'seq', axis=0, tiled=True)  41.3 us
    reduce_scatter x1, waiting for transfers between devices, body(): lax.psum_scatter(running, 'mp', scatter_dimension=1, tiled=True)  30.5 us
    all_gather x2, blocking collectives, entering(): lax.all_gather(part.astype(kind), axis)  19.8 us
    all_gather x1, blocking collectives, body(): lax.all_gather(w_in_out, 'seq', axis=0, tiled=True)  17.5 us
    all_gather x1, waiting for transfers between devices, body(): lax.all_gather(w_value, 'seq', axis=0, tiled=True)  16.9 us
    rev x1, local copies, waits for them, and re-layouts, body(): normalize(reverse_full)[:, ::-1] * norm_gain  15 us
  transfers between devices with their start and end apart: 13, of which 7 were waited for; matrix products, arithmetic and copies ran while one was open for 23% of the time, Pallas kernels for 0%

commit v1 on v0

--- a/solution.py
+++ b/solution.py
@@ -120,6 +120,18 @@
     conv_in_out,
     w_out,
 ):
+
+    def reach_the_column(message, shard_axis):
+        parts_n = lax.axis_size(shard_axis)
+        local_now = [(q - 1, q) for q in range(1, parts_n)] + [(parts_n - 1, 0)]
+        aux = message
+        crops = [aux]
+        for _ in range(parts_n - 1):
+            aux = lax.ppermute(aux, shard_axis, local_now)
+            crops += [aux]
+        last = jnp.concatenate([*reversed(crops)], axis=1)
+        return jnp.roll(last, (lax.axis_index(shard_axis) + 1) * aux.shape[1], axis=1)
+
     rows_local = hidden[0]
     segment = segment_ids[0]
     tok_count = rows_local.shape[0]
@@ -200,7 +212,7 @@
     normed = normed.reshape(2, tok_count, heads_local * head_width).astype(jnp.bfloat16)
     forward_mix = normed[0]
     reverse_mix = normed[1][::-1]
-    block_cols = lax.all_gather(w_out, "seq", axis=1, tiled=True)
+    block_cols = reach_the_column(w_out, "seq")
     direct = jnp.dot(forward_mix, block_cols, preferred_element_type=jnp.float32)
     flipped = jnp.dot(reverse_mix, block_cols, preferred_element_type=jnp.float32)[:, ::-1]
     running = direct

time: 403 us -> 394 us (0.978)
  waiting for transfers between devices: 191 us -> 79.2 us
  blocking collectives: 57.2 us -> 118 us
  starting transfers between devices: 15.6 us -> 38 us
  local copies, waits for them, and re-layouts: 64.4 us -> 77.2 us
  other arithmetic: 28.4 us -> 32.7 us
    all_gather x1 -> x0, waiting for transfers between devices: 50.7 us -> none  [body(): block_cols = lax.all_gather(w_out, 'seq', axis=1, tiled=True)]
    all_gather x1, waiting for transfers between devices: 41.3 us -> 0.02 us  [body(): lax.all_gather(w_gate, 'seq', axis=0, tiled=True)]
    all_gather x2, blocking collectives: 19.8 us -> 58.8 us  [entering(): lax.all_gather(part.astype(kind), axis)]
    ppermute x0 -> x3, waiting for transfers between devices: none -> 23.9 us  [reach_the_column(): aux = lax.ppermute(aux, shard_axis, local_now)]
    all_gather x2, waiting for transfers between devices: 45.4 us -> 22.4 us  [entering(): lax.all_gather(part.astype(kind), axis)]
    ppermute x0 -> x3, starting transfers between devices: none -> 22.7 us  [reach_the_column(): aux = lax.ppermute(aux, shard_axis, local_now)]
    all_gather x1, blocking collectives: 14.1 us -> 31.7 us  [body(): lax.all_gather(w_step, 'seq', axis=0, tiled=True)]
    all_gather x1, waiting for transfers between devices: 16.9 us -> 0.02 us  [body(): lax.all_gather(w_value, 'seq', axis=0, tiled=True)]
  transfers between devices with their start and end apart: 13 -> 15, of which waited for: 7 -> 3; matrix products, arithmetic and copies ran while one was open for 23% -> 20% of each run, Pallas kernels for 0% -> 0%
where the time goes in v1:
time: 394 us; the launch traced here: 390 us
  blocking collectives  118 us (30%)
  waiting for transfers between devices  79.2 us (20%)
  local copies, waits for them, and re-layouts  77.2 us (20%)
  starting transfers between devices  38 us (10%)
  other arithmetic  32.7 us (8%)
  matrix products  30.9 us (8%)
  between operations  14.2 us (4%)
    all_gather x2, blocking collectives, entering(): lax.all_gather(part.astype(kind), axis)  58.8 us
    all_gather x1, blocking collectives, body(): lax.all_gather(w_step, 'seq', axis=0, tiled=True)  31.7 us
    reduce_scatter x1, waiting for transfers between devices, body(): lax.psum_scatter(running, 'mp', scatter_dimension=1, tiled=True)  31.4 us
    ppermute x3, waiting for transfers between devices, reach_the_column(): aux = lax.ppermute(aux, shard_axis, local_now)  23.9 us
    ppermute x3, starting transfers between devices, reach_the_column(): aux = lax.ppermute(aux, shard_axis, local_now)  22.7 us
    all_gather x2, waiting for transfers between devices, entering(): lax.all_gather(part.astype(kind), axis)  22.4 us
    all_gather x1, blocking collectives, body(): lax.all_gather(w_in_out, 'seq', axis=0, tiled=True)  21.9 us
    rev x1, local copies, waits for them, and re-layouts, body(): normalize(reverse_full)[:, ::-1] * norm_gain  17.8 us
  transfers between devices with their start and end apart: 15, of which 3 were waited for; matrix products, arithmetic and copies ran while one was open for 20% of the time, Pallas kernels for 0%

profile of v1, /device:TPU:0, one launch (start us, length us, event | category | flops | bytes accessed | tf_op | source)
XLA Modules:
  0.0 390.3 jit_solution(7247557841557117803)
XLA Ops:
  9.3 5.5 %collective-permute-start.4 = (s32[1]{0:T(128)}, s32[1]{0:T(128)}, u32[]{:S(2)}, u32[]{:S(2)}) collective-permute-start(s32[1]{0:T(128)} %bitcast.30), channel_id=1, source_target_pairs={{0,4},{4,8},{8,12},{1,5},{5,9},{9,13},{2,6},{6,10},{10,14},{3,7},{... | collective-permute-start | bytes 20 | tf_op jit(solution)/shard_map/ppermute | solution.py:15
  14.8 1.3 collective-permute-start.5
  16.1 2.7 collective-permute-start.6
  19.9 31.7 %all_gather.38 = bf16[2048,16]{0,1:T(8,128)(2,1)S(1)} all-gather(bf16[512,16]{0,1:T(8,128)(2,1)S(1)} %copy-done.24), channel_id=1, replica_groups=mesh['groups'=2,'seq'=4,'mp'=2,'batch'=2] {'seq'}, dimensions={0}, use_global_device_ids=true | all-gather | bytes 81920 | tf_op jit(solution)/shard_map/all_gather | solution.py:149
  51.6 21.9 %all_gather.36 = bf16[2048,128]{1,0:T(8,128)(2,1)} all-gather(bf16[512,128]{1,0:T(8,128)(2,1)S(1)} %copy-done.18), channel_id=1, replica_groups=mesh['groups'=2,'seq'=4,'mp'=2,'batch'=2] {'seq'}, dimensions={0}, use_global_device_ids=true | all-gather | bytes 655360 | tf_op jit(solution)/shard_map/all_gather | solution.py:148
  74.2 1.5 fusion.45
  75.7 1.4 pad_add_fusion.1
  77.2 12.6 %rev.13 = bf16[256,2048]{1,0:T(8,128)(2,1)S(1)} reverse(bf16[256,2048]{1,0:T(8,128)(2,1)} %bitcast.137), dimensions={0} | reverse | bytes 2097152 | tf_op jit(solution)/shard_map/rev | solution.py:140
  90.1 1.6 convert_multiply_fusion.1
  91.8 17.8 %rev.14 = f32[256,2048]{1,0:T(8,128)} reverse(f32[256,2048]{1,0:T(8,128)} %convert_multiply_fusion.1), dimensions={1} | reverse | bytes 4194304 | tf_op jit(solution)/shard_map/rev | solution.py:143
  109.8 2.2 fusion.18
  114.1 2.3 convolution_convert_fusion.2
  116.4 1.6 collective-permute-start.2
  117.9 1.3 collective-permute-start.3
  123.7 4.1 %collective-permute-start.7 = (bf16[1024,512]{1,0:T(8,128)(2,1)S(1)}, bf16[1024,512]{1,0:T(8,128)(2,1)}, u32[]{:S(2)}, u32[]{:S(2)}) collective-permute-start(bf16[1024,512]{1,0:T(8,128)(2,1)S(1)} %collective-permute-done.6), channel_id=1, source_target_pairs={{0,4},{4,8},{8,12},{12,0},{1,5},{5,9},{9,13},{13,1},{2,6},{6,10},{... | collective-permute-start | bytes 3145736 | tf_op jit(solution)/shard_map/ppermute | solution.py:130
  128.8 5.1 %convolution_convert_fusion.1 = bf16[512,1024]{1,0:T(8,128)(2,1)S(1)} fusion(bf16[2048,1024]{1,0:T(8,128)(2,1)} %all-gather.9.cloned.1.call-done, bf16[256,2048]{1,0:T(8,128)(2,1)} %copy-done.11, bf16[256,2048]{1,0:T(8,128)(2,1)S(1)} %copy-done.9), kind=kOutput, calls=%fused_computation.48 | convolution fusion | flops 2152202240 | bytes 7340032 | tf_op jit(solution)/shard_map/dot_general | solution.py:152
  133.9 4.0 %collective-permute-start = (bf16[3,1024]{1,0:T(4,128)(2,1)S(1)}, bf16[3,1024]{1,0:T(4,128)(2,1)S(1)}, u32[]{:S(2)}, u32[]{:S(2)}) collective-permute-start(bf16[3,1024]{1,0:T(4,128)(2,1)S(1)} %get-tuple-element.314), channel_id=1, source_target_pairs={{0,4},{4,8},{8,12},{1,5},{5,9},{9,13},{2,6},{6,10},{10,14},{3,7},{... | collective-permute-start | bytes 18440 | tf_op jit(solution)/shard_map/ppermute | solution.py:26
  137.9 1.3 collective-permute-start.1
  139.2 5.7 %all_gather.37 = bf16[2,256,256]{2,1,0:T(8,128)(2,1)S(1)} all-gather(bf16[2,256,128]{2,1,0:T(8,128)(2,1)S(1)} %multiply_convert_fusion.9), channel_id=1, replica_groups=mesh['groups'=2,'seq'=4,'mp'=2,'batch'=2] {'mp'}, dimensions={2}, use_global_device_ids=true | all-gather | bytes 393216 | tf_op jit(solution)/shard_map/all_gather | solution.py:166
  144.8 23.9 %collective-permute-done.7 = bf16[1024,512]{1,0:T(8,128)(2,1)} collective-permute-done((bf16[1024,512]{1,0:T(8,128)(2,1)S(1)}, bf16[1024,512]{1,0:T(8,128)(2,1)}, u32[]{:S(2)}, u32[]{:S(2)}) %collective-permute-start.7) | collective-permute-done | bytes 1048608 | tf_op jit(solution)/shard_map/ppermute | solution.py:130
  168.7 15.9 %collective-permute-start.8 = (bf16[1024,512]{1,0:T(8,128)(2,1)}, bf16[1024,512]{1,0:T(8,128)(2,1)}, u32[]{:S(2)}, u32[]{:S(2)}) collective-permute-start(bf16[1024,512]{1,0:T(8,128)(2,1)} %collective-permute-done.7), channel_id=1, source_target_pairs={{0,4},{4,8},{8,12},{12,0},{1,5},{5,9},{9,13},{13,1},{2,6},{6,10},{... | collective-permute-start | bytes 3145736 | tf_op jit(solution)/shard_map/ppermute | solution.py:130
  186.2 1.3 copy.85
  187.5 1.7 fusion.28
  190.1 50.6 %all-gather.1 = bf16[4,1,16]{2,1,0:T(2,128)(2,1)S(1)} all-gather(bf16[1,1,16]{2,1,0:T(2,128)(2,1)S(1)} %get-tuple-element.338), channel_id=3, replica_groups=mesh['groups'=2,'seq'=4,'mp'=2,'batch'=2] {'seq'}, dimensions={0}, use_global_device_ids=true | all-gather | bytes 160 | tf_op jit(solution)/shard_map/all_gather | solution.py:32
  240.8 8.1 %all-gather.2 = bf16[4,1,16]{2,1,0:T(2,128)(2,1)S(1)} all-gather(bf16[1,1,16]{2,1,0:T(2,128)(2,1)S(1)} %get-tuple-element.339), channel_id=4, replica_groups=mesh['groups'=2,'seq'=4,'mp'=2,'batch'=2] {'seq'}, dimensions={0}, use_global_device_ids=true | all-gather | bytes 160 | tf_op jit(solution)/shard_map/all_gather | solution.py:32
  250.1 1.4 constant_dynamic-update-slice_fusion.7
  251.4 1.5 constant_dynamic-update-slice_fusion.6
  253.2 1.4 constant_dynamic-update-slice_fusion.3
  254.6 1.4 constant_dynamic-update-slice_fusion.2
  256.4 3.3 copy-done.5
  259.9 5.8 %convolution_convert_fusion = bf16[512,1024]{1,0:T(8,128)(2,1)} fusion(bf16[2048,1024]{1,0:T(8,128)(2,1)} %all-gather.15.cloned.1.call-done, bf16[256,2048]{1,0:T(8,128)(2,1)} %copy-done.11, bf16[256,2048]{1,0:T(8,128)(2,1)S(1)} %copy-done.10), kind=kOutput, calls=%fused_computation.47 | convolution fusion | flops 2152202240 | bytes 7340032 | tf_op jit(solution)/shard_map/dot_general | solution.py:152
  265.8 1.6 copy.94
  267.4 4.5 %while.37 = (s32[]{:T(128)}, f32[16,64,128]{2,1,0:T(8,128)S(1)}, s32[]{:T(128)}, bf16[4,16]{1,0:T(4,128)(2,1)S(1)}, bf16[4,16,64,128]{3,2,1,0:T(8,128)(2,1)}, /*index=5*/s32[]{:T(128)}, s32[]{:T(128)}) while((s32[]{:T(128)}, f32[16,64,128]{2,1,0:T(8,128)S(1)}, s32[]{:T(128)}, bf16[4,16]{1,0:T(4,128)(2,1)S(1)}, ...), condition=%wide.region_5.6_spmd.clone, body=%wide.region_4.5_spmd.clone.sunk | while | flops 655380 | bytes 1310993 | solution.py:50
  271.9 22.4 %all-gather.13.cloned.1.call-done = bf16[4,16,64,128]{3,2,1,0:T(8,128)(2,1)} async-done(((bf16[1,16,64,128]{3,2,1,0:T(8,128)(2,1)}), bf16[4,16,64,128]{3,2,1,0:T(8,128)(2,1)}) %all-gather.13.cloned.1.call-update) | async-done | bytes 1048592 | tf_op jit(solution)/shard_map/all_gather | solution.py:32
  294.3 4.5 %while.38 = (s32[]{:T(128)}, f32[16,64,128]{2,1,0:T(8,128)S(1)}, s32[]{:T(128)}, bf16[4,16]{1,0:T(4,128)(2,1)S(1)}, bf16[4,16,64,128]{3,2,1,0:T(8,128)(2,1)}, /*index=5*/s32[]{:T(128)}, s32[]{:T(128)}, s32[]{:T(128)}, s32[]{:T(128)}) while((s32[]{:T(128)}, f32[16,64,128]{2,1,0:T(8,128)S(1)}, s32[]{:T(128)}, ...), condition=%wide.region_7.8_spmd.clone, body=%wide.region_6.7_spmd.clone.sunk | while | flops 655384 | bytes 1311055 | solution.py:50
  300.9 4.2 %fusion.27 = f32[2,1,256,16,64]{2,4,3,0,1:T(8,128)} fusion(f32[2,1,256,16,64]{2,4,3,0,1:T(8,128)S(1)} %bitcast.140, f32[2,256,16,64]{1,3,2,0:T(8,128)S(1)} %fusion.30, bf16[2,256,16,64]{1,3,2,0:T(8,128)(2,1)S(1)} %bitcast.145, f32[2,16,256]{2,1,0:T(8,128)S(1)} %copy-done.22, f32[2,16,256]{2,1,0:T(8,128)S(1)} %reduce_window_sum.30, ...), kind=kOutput, calls=%fused_computation.42 | convolution fusion | flops 283115520 | bytes 8093760 | tf_op jit(solution)/shard_map/vmap(vmap(hij,jhp->ihp))/dot_general | solution.py:64
  305.1 2.0 copy.95
  307.2 1.9 fusion.54
  309.1 4.0 %mul.396 = f32[2,256,2,512]{3,2,1,0:T(2,128)} reshape(f32[2,256,1024]{2,1,0:T(8,128)} %fusion.54) | data formatting | bytes 4194304 | tf_op jit(solution)/shard_map/mul | solution.py:211
  313.1 2.2 reduce_sum.29
  315.4 1.7 mul.397
  317.1 4.0 %mul.398 = f32[2,256,1024]{2,1,0:T(8,128)} reshape(f32[2,256,2,512]{3,2,1,0:T(2,128)} %mul.397) | data formatting | bytes 4194304 | tf_op jit(solution)/shard_map/mul | solution.py:211
  321.2 2.4 multiply_convert_fusion.2
  325.2 4.8 %fusion.9 = f32[256,2048]{1,0:T(8,128)} fusion(bf16[256,1024]{1,0:T(8,128)(2,1)S(1)} %rev.15, bf16[1024,4096]{1,0:T(8,128)(2,1)} %copy-done.5, s32[]{:T(128)S(6)} %select_n.98), kind=kOutput, calls=%fused_computation.14 | convolution fusion | flops 1073741824 | bytes 6815748 | tf_op jit(solution)/shard_map/dot_general | solution.py:217
  330.1 15.0 %rev.16 = f32[256,2048]{1,0:T(8,128)S(1)} reverse(f32[256,2048]{1,0:T(8,128)} %fusion.9), dimensions={1} | reverse | bytes 4194304 | tf_op jit(solution)/shard_map/rev | solution.py:217
  345.1 4.9 %fusion.13 = f32[256,2048]{1,0:T(8,128)} fusion(f32[256,2048]{1,0:T(8,128)S(1)} %rev.16, bf16[1024,4096]{1,0:T(8,128)(2,1)} %copy-done.5, s32[]{:T(128)S(6)} %select_n.98, bf16[2,256,1024]{2,1,0:T(8,128)(2,1)S(1)} %copy-done.4), kind=kOutput, calls=%fused_computation.24 | convolution fusion | flops 1074266112 | bytes 8912900 | tf_op jit(solution)/shard_map/dot_general | solution.py:216
  350.0 31.4 %reduce-scatter.2.cloned.1.call-done = f32[256,1024]{1,0:T(8,128)} async-done(((f32[256,2048]{1,0:T(8,128)}), f32[256,1024]{1,0:T(8,128)}) %reduce-scatter.2.cloned.1.call-update) | async-done | bytes 1048592 | tf_op jit(solution)/shard_map/reduce_scatter | solution.py:220
  381.3 2.1 convert_bitcast_fusion
  (162 shorter events, 29.6 us)
Async XLA Ops:
  6.5 12.4 %copy-start.25 = (s32[1,256]{1,0:T(1,128)S(1)}, s32[1,256]{1,0:T(1,128)}, u32[]{:S(2)}) copy-start(s32[1,256]{1,0:T(1,128)} %param.18) | copy-start | bytes 3076
  6.5 12.5 %copy-start.28 = (bf16[4,128]{1,0:T(4,128)(2,1)S(1)}, bf16[4,128]{1,0:T(4,128)(2,1)}, u32[]{:S(2)}) copy-start(bf16[4,128]{1,0:T(4,128)(2,1)} %param.28) | copy-start | bytes 3076
  6.5 13.3 %copy-start.20 = (bf16[4,1024]{1,0:T(4,128)(2,1)S(1)}, bf16[4,1024]{1,0:T(4,128)(2,1)}, u32[]{:S(2)}) copy-start(bf16[4,1024]{1,0:T(4,128)(2,1)} %param.27) | copy-start | bytes 24580
  6.5 13.3 %copy-start.24 = (bf16[512,16]{0,1:T(8,128)(2,1)S(1)}, bf16[512,16]{0,1:T(8,128)(2,1)}, u32[]{:S(2)}) copy-start(bf16[512,16]{0,1:T(8,128)(2,1)} %param.23) | copy-start | bytes 49156
  6.5 45.0 %copy-start.18 = (bf16[512,128]{1,0:T(8,128)(2,1)S(1)}, bf16[512,128]{1,0:T(8,128)(2,1)}, u32[]{:S(2)}) copy-start(bf16[512,128]{1,0:T(8,128)(2,1)} %param.22) | copy-start | bytes 393220
  6.5 70.7 %all-gather.17.cloned.1.call-start = ((), (), s32[]{:S(2)}) async-start(), calls=%async_computation.6 | async-start | bytes 1572864 | tf_op jit(solution)/shard_map/all_gather | solution.py:139
  7.3 121.5 %all-gather.9.cloned.1.call-start = ((), (), s32[]{:S(2)}) async-start(), calls=%async_computation.1 | async-start | bytes 5242880 | tf_op jit(solution)/shard_map/all_gather | solution.py:147
  8.0 251.9 %all-gather.15.cloned.1.call-start = ((), (), s32[]{:S(2)}) async-start(), calls=%async_computation.4 | async-start | bytes 5242880 | tf_op jit(solution)/shard_map/all_gather | solution.py:146
  9.3 64.9 %collective-permute-start.4 = (s32[1]{0:T(128)}, s32[1]{0:T(128)}, u32[]{:S(2)}, u32[]{:S(2)}) collective-permute-start(s32[1]{0:T(128)} %bitcast.30), channel_id=1, source_target_pairs={{0,4},{4,8},{8,12},{1,5},{5,9},{9,13},{2,6},{6,10},{10,14},{3,7},{... | collective-permute-start | bytes 20 | tf_op jit(solution)/shard_map/ppermute | solution.py:15
  14.8 59.4 %collective-permute-start.5 = (s32[1]{0:T(128)}, s32[1]{0:T(128)}, u32[]{:S(2)}, u32[]{:S(2)}) collective-permute-start(s32[1]{0:T(128)} %bitcast.31), channel_id=1, source_target_pairs={{4,0},{8,4},{12,8},{5,1},{9,5},{13,9},{6,2},{10,6},{14,10},{7,3},{... | collective-permute-start | bytes 20 | tf_op jit(solution)/shard_map/ppermute | solution.py:18
  16.1 107.7 %collective-permute-start.6 = (bf16[1024,512]{1,0:T(8,128)(2,1)}, bf16[1024,512]{1,0:T(8,128)(2,1)S(1)}, u32[]{:S(2)}, u32[]{:S(2)}) collective-permute-start(bf16[1024,512]{1,0:T(8,128)(2,1)} %param.29), channel_id=1, source_target_pairs={{0,4},{4,8},{8,12},{12,0},{1,5},{5,9},{9,13},{13,1},{2,6},{6,10},{... | collective-permute-start | bytes 3145736 | tf_op jit(solution)/shard_map/ppermute | solution.py:130
  18.8 248.6 %all-gather.11.cloned.1.call-start = ((), (), s32[]{:S(2)}) async-start(), calls=%async_computation.2 | async-start | bytes 1310720 | tf_op jit(solution)/shard_map/all_gather | solution.py:32
  91.8 17.8 %copy-start = (bf16[1,256,2048]{2,1,0:T(8,128)(2,1)S(1)}, bf16[1,256,2048]{2,1,0:T(8,128)(2,1)}, u32[]{:S(2)}) copy-start(bf16[1,256,2048]{2,1,0:T(8,128)(2,1)} %all-gather.17.cloned.1.call-done) | copy-start | bytes 3145732
  91.8 18.1 %copy-start.26 = (f32[2048]{0:T(1024)S(1)}, f32[2048]{0:T(1024)}, u32[]{:S(2)}) copy-start(f32[2048]{0:T(1024)} %param.19) | copy-start | bytes 24580
  112.0 1.0 copy-start.8
  112.0 1.3 copy-start.11
  112.0 2.0 copy-start.12
  114.1 5.2 %copy-start.29 = (f32[16]{0:T(128)S(1)}, f32[16]{0:T(128)}, u32[]{:S(2)}) copy-start(f32[16]{0:T(128)} %param.24) | copy-start | bytes 196
  114.1 5.2 %copy-start.31 = (f32[16]{0:T(128)S(1)}, f32[16]{0:T(128)}, u32[]{:S(2)}) copy-start(f32[16]{0:T(128)} %param.25) | copy-start | bytes 196
  116.3 12.4 %copy-start.9 = (bf16[256,2048]{1,0:T(8,128)(2,1)S(1)}, bf16[256,2048]{1,0:T(8,128)(2,1)}, u32[]{:S(2)}) copy-start(bf16[256,2048]{1,0:T(8,128)(2,1)} %copy-done.8) | copy-start | bytes 3145732
  116.4 11.5 %collective-permute-start.2 = (bf16[3,128]{1,0:T(4,128)(2,1)S(1)}, bf16[3,128]{1,0:T(4,128)(2,1)S(1)}, u32[]{:S(2)}, u32[]{:S(2)}) collective-permute-start(bf16[3,128]{1,0:T(4,128)(2,1)S(1)} %get-tuple-element.318), channel_id=1, source_target_pairs={{0,4},{4,8},{8,12},{1,5},{5,9},{9,13},{2,6},{6,10},{10,14},{3,7},{... | collective-permute-start | bytes 2312 | tf_op jit(solution)/shard_map/ppermute | solution.py:26
  117.9 9.9 %collective-permute-start.3 = (bf16[3,128]{1,0:T(4,128)(2,1)S(1)}, bf16[3,128]{1,0:T(4,128)(2,1)S(1)}, u32[]{:S(2)}, u32[]{:S(2)}) collective-permute-start(bf16[3,128]{1,0:T(4,128)(2,1)S(1)} %get-tuple-element.319), channel_id=1, source_target_pairs={{4,0},{8,4},{12,8},{5,1},{9,5},{13,9},{6,2},{10,6},{14,10},{7,3},{... | collective-permute-start | bytes 2312 | tf_op jit(solution)/shard_map/ppermute | solution.py:26
  120.6 13.3 %copy-start.14 = (f32[2,1,16,2,128]{4,2,3,1,0:T(8,128)}, f32[2,1,16,2,128]{4,2,3,1,0:T(8,128)S(1)}, u32[]{:S(2)}) copy-start(f32[2,1,16,2,128]{4,2,3,1,0:T(8,128)S(1)} %reduce-window.6) | copy-start | bytes 98308
  121.0 12.9 %copy-start.16 = (f32[2,16,2,128]{3,2,1,0:T(2,128)}, f32[2,16,2,128]{3,2,1,0:T(2,128)S(1)}, u32[]{:S(2)}) copy-start(f32[2,16,2,128]{3,2,1,0:T(2,128)S(1)} %broadcast.225) | copy-start | bytes 98308
  123.7 45.0 %collective-permute-start.7 = (bf16[1024,512]{1,0:T(8,128)(2,1)S(1)}, bf16[1024,512]{1,0:T(8,128)(2,1)}, u32[]{:S(2)}, u32[]{:S(2)}) collective-permute-start(bf16[1024,512]{1,0:T(8,128)(2,1)S(1)} %collective-permute-done.6), channel_id=1, source_target_pairs={{0,4},{4,8},{8,12},{12,0},{1,5},{5,9},{9,13},{13,1},{2,6},{6,10},{... | collective-permute-start | bytes 3145736 | tf_op jit(solution)/shard_map/ppermute | solution.py:130
  133.9 50.7 %collective-permute-start = (bf16[3,1024]{1,0:T(4,128)(2,1)S(1)}, bf16[3,1024]{1,0:T(4,128)(2,1)S(1)}, u32[]{:S(2)}, u32[]{:S(2)}) collective-permute-start(bf16[3,1024]{1,0:T(4,128)(2,1)S(1)} %get-tuple-element.314), channel_id=1, source_target_pairs={{0,4},{4,8},{8,12},{1,5},{5,9},{9,13},{2,6},{6,10},{10,14},{3,7},{... | collective-permute-start | bytes 18440 | tf_op jit(solution)/shard_map/ppermute | solution.py:26
  137.9 46.7 %collective-permute-start.1 = (bf16[3,1024]{1,0:T(4,128)(2,1)S(1)}, bf16[3,1024]{1,0:T(4,128)(2,1)S(1)}, u32[]{:S(2)}, u32[]{:S(2)}) collective-permute-start(bf16[3,1024]{1,0:T(4,128)(2,1)S(1)} %get-tuple-element.315), channel_id=1, source_target_pairs={{4,0},{8,4},{12,8},{5,1},{9,5},{13,9},{6,2},{10,6},{14,10},{7,3},{... | collective-permute-start | bytes 18440 | tf_op jit(solution)/shard_map/ppermute | solution.py:26
  168.7 81.4 %collective-permute-start.8 = (bf16[1024,512]{1,0:T(8,128)(2,1)}, bf16[1024,512]{1,0:T(8,128)(2,1)}, u32[]{:S(2)}, u32[]{:S(2)}) collective-permute-start(bf16[1024,512]{1,0:T(8,128)(2,1)} %collective-permute-done.7), channel_id=1, source_target_pairs={{0,4},{4,8},{8,12},{12,0},{1,5},{5,9},{9,13},{13,1},{2,6},{6,10},{... | collective-permute-start | bytes 3145736 | tf_op jit(solution)/shard_map/ppermute | solution.py:130
  186.2 1.4 copy-start.23
  186.2 1.3 copy-start.30
  187.5 2.6 copy-start.27
  187.5 61.4 %copy-start.17 = (f32[2,16,2,128]{3,2,1,0:T(2,128)S(1)}, f32[2,16,2,128]{3,2,1,0:T(2,128)}, u32[]{:S(2)}) copy-start(f32[2,16,2,128]{3,2,1,0:T(2,128)} %copy-done.16) | copy-start | bytes 98308
  187.5 61.4 %copy-start.15 = (f32[2,1,16,2,128]{4,2,3,1,0:T(8,128)S(1)}, f32[2,1,16,2,128]{4,2,3,1,0:T(8,128)}, u32[]{:S(2)}) copy-start(f32[2,1,16,2,128]{4,2,3,1,0:T(8,128)} %copy-done.14) | copy-start | bytes 98308
  190.1 104.3 %all-gather.13.cloned.1.call-start = ((), (), s32[]{:S(2)}) async-start(), calls=%async_computation.3 | async-start | bytes 1310720 | tf_op jit(solution)/shard_map/all_gather | solution.py:32
  251.4 1.6 copy-start.1
  256.2 3.7 copy-start.10
  256.3 3.3 copy-start.5
  259.7 121.7 %reduce-scatter.2.cloned.1.call-start = ((), (), s32[]{:S(2)}) async-start(), calls=%async_computation.5 | async-start | bytes 3145728 | tf_op jit(solution)/shard_map/reduce_scatter | solution.py:220
  298.9 1.6 copy-start.6
  298.9 1.8 copy-start.7
  298.9 2.0 copy-start.13
  298.9 2.0 copy-start.19
  298.9 2.0 copy-start.21
  298.9 2.0 copy-start.22
  298.9 2.0 copy-start.32
  305.1 2.0 copy-start.2
  323.5 1.0 copy-start.3
  330.1 15.0 %copy-start.4 = (bf16[2,256,1024]{2,1,0:T(8,128)(2,1)S(1)}, bf16[2,256,1024]{2,1,0:T(8,128)(2,1)}, u32[]{:S(2)}) copy-start(bf16[2,256,1024]{2,1,0:T(8,128)(2,1)} %copy-done.3) | copy-start | bytes 3145732
Sparse Core Ops, SparseCore 0:
  8.9 23.9 all-gather.16
  34.5 89.5 all-gather.8
  125.7 112.1 all-gather.14
  239.3 26.1 all-gather.10
  266.9 27.4 all-gather.12
  350.1 31.1 reduce-scatter.1
